TPU v7x, 32 devices: a whole 2x2x4 slice. The times are simulated.
32 devices in a mesh: groups: 2 (over y), seq: 4 (over z), head: 2 (over x), rep: 2 (over core).
Axes of the slice: x: 2, y: 2, z: 4, core: 2. Of those that a mesh axis runs over, the one named last changes fastest.
Arguments:
- queries: bfloat16 [8192, 2048], P(('groups', 'seq'), ('head', 'rep')), parts along dimension 0, may hold values from -8 to 8
- keys_values: bfloat16 [2, 8192, 2048], P(None, ('groups', 'seq'), ('head', 'rep')), parts along dimension 1, may hold values from -8 to 8
- pack_pos: int32 [1024], P('groups'), parts along dimension 0, may hold values from 0 to 4095
- bounds: int32 [2, 8192], P(None, ('groups', 'seq')), parts along dimension 1, may hold values from 0 to 4096, as said below
- radius: int32 [32], P(('head', 'rep')), may hold values from 128 to 512, as said below
- pack_proj: bfloat16 [2, 2048, 2048], P(None, None, ('head', 'rep')), may hold values from -0.5 to 0.5
Outputs:
- mixed: bfloat16 [8192, 2048], P(('groups', 'seq'), ('head', 'rep')), parts along dimension 0
There are 2 independent parts, one for each index of `groups`. A program takes and returns all parts, laid end to end along the dimension named above; an argument that names none is the same for every part. Nothing has to cross between parts.
Inputs may be any that keep to these rules, and one draw needn't show every extreme that they name: bounds[0, s] and bounds[1, s] are the first position and the end (exclusive) of the document of token s; the 8 documents are contiguous and tile the sequence. Some head has radius exactly 512.
All inputs are finite; a program needn't handle non-finite values.
Results may differ from a plain program's by a relative error of at most 0.012.
Values may be sent and summed in bfloat16 or wider, within the bound.
A program may use at most 128 MiB of HBM per device.

v0:
```python
import math
import jax
import jax.numpy as jnp
from jax import lax
from jax.sharding import PartitionSpec as P

HEAD_DIM = 64
PACK = 512
RADIUS = 512


def padded(cells, sides, width):
    for axis, dim in sides:
        count = lax.axis_size(axis)
        ends = count - 1
        head = lax.slice_in_dim(cells, 0, width, axis=dim)
        tail = lax.slice_in_dim(cells, cells.shape[dim] - width, cells.shape[dim], axis=dim)
        cells = jnp.concatenate(
            [
                lax.ppermute(tail, axis, [(i, (i + 1) % count) for i in range(ends)]),
                cells,
                lax.ppermute(head, axis, [((i + 1) % count, i) for i in range(ends)]),
            ],
            axis=dim,
        )
    return cells


def divide_heads(summed, totals):
    rows_here, heads_here = totals.shape
    shaped = summed.reshape(rows_here, heads_here, -1) / totals[:, :, None]
    return shaped.reshape(rows_here, -1)


def attend(
    query_block,
    window_keys,
    window_values,
    pack_key_heads,
    pack_value_heads,
    lower,
    upper,
    radius,
    first_pos,
):
    rows_here = query_block.shape[0]
    window_len = window_keys.shape[0]
    scale = 1.0 / math.sqrt(HEAD_DIM)
    pack_scores = (
        jnp.einsum("qhd,phd->hqp", query_block, pack_key_heads, preferred_element_type=jnp.float32)
        * scale
    )
    window_scores = (
        jnp.einsum("qhd,khd->hqk", query_block, window_keys, preferred_element_type=jnp.float32)
        * scale
    )
    query_pos = first_pos + jnp.arange(rows_here, dtype=jnp.int32)
    key_pos = first_pos - RADIUS + jnp.arange(window_len, dtype=jnp.int32)
    distance = jnp.abs(key_pos[None, :] - query_pos[:, None])
    inside = (key_pos[None, :] >= lower[:, None]) & (key_pos[None, :] < upper[:, None])
    allowed = (distance[None, :, :] <= radius[:, None, None]) & inside[None, :, :]
    window_scores = jnp.where(allowed, window_scores, -1e30)
    highest = jnp.maximum(jnp.max(pack_scores, axis=2), jnp.max(window_scores, axis=2))
    pack_weights = jnp.exp(pack_scores - highest[:, :, None])
    window_weights = jnp.exp(window_scores - highest[:, :, None])
    totals = jnp.sum(pack_weights, axis=2) + jnp.sum(window_weights, axis=2)
    summed = jnp.einsum(
        "hqp,phd->qhd",
        pack_weights.astype(jnp.bfloat16),
        pack_value_heads,
        preferred_element_type=jnp.float32,
    )
    summed = summed + jnp.einsum(
        "hqk,khd->qhd",
        window_weights.astype(jnp.bfloat16),
        window_values,
        preferred_element_type=jnp.float32,
    )
    return (summed / totals.T[:, :, None]).reshape(rows_here, -1).astype(jnp.bfloat16)


def shards(queries, keys_values, pack_pos, bounds, radius, pack_proj):
    tokens_here, width = queries.shape
    heads_here = radius.shape[0]
    scale = 1.0 / math.sqrt(HEAD_DIM)
    offset_pos = lax.axis_index("seq") * tokens_here
    local_pos = pack_pos - offset_pos
    selector = (local_pos[:, None] == jnp.arange(tokens_here, dtype=jnp.int32)[None, :]).astype(
        jnp.bfloat16
    )
    picked = jnp.dot(selector, queries, preferred_element_type=jnp.float32)
    picked_share = lax.psum_scatter(
        picked.astype(jnp.bfloat16), "seq", scatter_dimension=0, tiled=True
    )
    pack_query = lax.all_gather(picked_share, "seq", axis=0, tiled=True)
    query_heads = pack_query.reshape(PACK, heads_here, HEAD_DIM)
    key_heads = keys_values[0].reshape(tokens_here, heads_here, HEAD_DIM)
    value_heads = keys_values[1].reshape(tokens_here, heads_here, HEAD_DIM)
    pack_scores = (
        jnp.einsum("phd,thd->pht", query_heads, key_heads, preferred_element_type=jnp.float32)
        * scale
    )
    local_top = jnp.max(pack_scores, axis=2)
    global_top = lax.pmax(local_top, "seq")
    pack_weights = jnp.exp(pack_scores - global_top[:, :, None])
    row_total = jnp.sum(pack_weights, axis=2)
    row_sum = jnp.einsum(
        "pht,thd->phd",
        pack_weights.astype(jnp.bfloat16),
        value_heads,
        preferred_element_type=jnp.float32,
    ).reshape(PACK, width)
    whole_sum, whole_total = lax.psum((row_sum, row_total), "seq")
    packed = divide_heads(whole_sum, whole_total).astype(jnp.bfloat16)
    portion = lax.all_gather(packed, ("head", "rep"), axis=1, tiled=True)
    key_part = jnp.dot(portion, pack_proj[0], preferred_element_type=jnp.float32)
    value_part = jnp.dot(portion, pack_proj[1], preferred_element_type=jnp.float32)
    pack_keys = key_part.astype(jnp.bfloat16)
    pack_values = value_part.astype(jnp.bfloat16)
    extended = padded(keys_values, (("seq", 1),), RADIUS)
    rows_per = math.gcd(tokens_here, 512)
    window_len = rows_per + 2 * RADIUS
    pack_key_heads = pack_keys.reshape(PACK, heads_here, HEAD_DIM)
    pack_value_heads = pack_values.reshape(PACK, heads_here, HEAD_DIM)

    def token_block(which_block):
        offset_row = which_block * rows_per
        query_block = lax.dynamic_slice_in_dim(queries, offset_row, rows_per, 0).reshape(
            rows_per, heads_here, HEAD_DIM
        )
        window = lax.dynamic_slice_in_dim(extended, offset_row, window_len, 1)
        window_keys = window[0].reshape(window_len, heads_here, HEAD_DIM)
        window_values = window[1].reshape(window_len, heads_here, HEAD_DIM)
        lower = lax.dynamic_slice_in_dim(bounds[0], offset_row, rows_per, 0)
        upper = lax.dynamic_slice_in_dim(bounds[1], offset_row, rows_per, 0)
        return attend(
            query_block,
            window_keys,
            window_values,
            pack_key_heads,
            pack_value_heads,
            lower,
            upper,
            radius,
            offset_pos + offset_row,
        )

    blocks_out = lax.map(token_block, jnp.arange(tokens_here // rows_per, dtype=jnp.int32))
    return blocks_out.reshape(tokens_here, width)


def solution(mesh):
    return jax.shard_map(
        shards,
        mesh=mesh,
        in_specs=(
            P(("groups", "seq"), ("head", "rep")),
            P(None, ("groups", "seq"), ("head", "rep")),
            P("groups"),
            P(None, ("groups", "seq")),
            P(("head", "rep")),
            P(None, None, ("head", "rep")),
        ),
        out_specs=P(("groups", "seq"), ("head", "rep")),
        check_vma=False,
    )
```

profile of v0, /device:TPU:0, one launch (start us, length us, event | category | flops | bytes accessed | tf_op | source)
XLA Modules:
  0.0 283.8 jit_solution(12413389611932709694)
XLA Ops:
  6.5 0.7 broadcast_subtract_fusion
  7.2 2.8 fusion.35
  10.0 0.0 reduce-scatter.2.cloned.1.call-update
  10.0 0.0 all-reduce.2.cloned.1.call-start
  10.1 1.7 fusion.48
  11.8 0.5 copy.19
  12.3 0.5 copy.18
  12.8 21.7 %reduce-scatter.2.cloned.1.call-done = bf16[128,512]{1,0:T(8,128)(2,1)} async-done(((bf16[512,512]{1,0:T(8,128)(2,1)}), bf16[128,512]{1,0:T(8,128)(2,1)}) %reduce-scatter.2.cloned.1.call-update) | async-done | bytes 131088 | tf_op jit(solution)/shard_map/reduce_scatter | solution.py:92
  34.5 16.1 %all_gather.6 = bf16[512,512]{1,0:T(8,128)(2,1)S(1)} all-gather(bf16[128,512]{1,0:T(8,128)(2,1)} %reduce-scatter.2.cloned.1.call-done), channel_id=1, replica_groups=mesh['groups'=2,'seq'=4,'head'=2,'rep'=2] {'seq'}, dimensions={0}, use_global_device_ids=true | all-gather | bytes 655360 | tf_op jit(solution)/shard_map/all_gather | solution.py:95
  50.6 0.2 copy.17
  50.8 8.1 %bitcast_reduce_fusion = (f32[512,8]{0,1:T(8,128)S(1)}, f32[8,512,1024]{2,1,0:T(8,128)}) fusion(bf16[512,8,64]{0,2,1:T(8,128)(2,1)S(1)} %bitcast.103, bf16[1024,8,64]{0,2,1:T(8,128)(2,1)S(1)} %bitcast.102), kind=kOutput, calls=%fused_computation.30 | convolution fusion | flops 545255424 | bytes 18366464 | tf_op jit(solution)/shard_map/phd,thd->pht/dot_general | solution.py:100
  58.9 15.9 %pmax.7 = f32[512,8]{0,1:T(8,128)S(1)} all-reduce(f32[512,8]{0,1:T(8,128)S(1)} %get-tuple-element.185), channel_id=1, replica_groups=mesh['groups'=2,'seq'=4,'head'=2,'rep'=2] {'seq'}, use_global_device_ids=true, to_apply=%region_2.0 | all-reduce | flops 4096 | bytes 32768 | tf_op jit(solution)/shard_map/pmax | solution.py:104
  74.8 8.2 %fusion.26 = f32[8,512,64]{1,2,0:T(8,128)} fusion(bf16[1024,8,64]{0,2,1:T(8,128)(2,1)S(1)} %bitcast.100, f32[8,512,1024]{2,1,0:T(8,128)} %get-tuple-element.186, f32[512,8]{0,1:T(8,128)S(1)} %pmax.7), kind=kOutput, calls=%fused_computation.34 | convolution fusion | flops 549453824 | bytes 18890752 | tf_op jit(solution)/shard_map/pht,thd->phd/dot_general | solution.py:107
  83.0 0.0 all-reduce.2.cloned.1.call-update
  83.0 0.0 all-gather.2.cloned.1.call-start
  83.0 7.6 %fusion.24 = f32[512,8]{0,1:T(8,128)S(1)} fusion(f32[8,512,1024]{2,1,0:T(8,128)} %get-tuple-element.186, f32[512,8]{0,1:T(8,128)S(1)} %pmax.7), kind=kLoop, calls=%fused_computation.32 | loop fusion | flops 12578816 | bytes 16809984 | tf_op jit(solution)/shard_map/reduce_sum | solution.py:106
  90.7 17.0 %psum.15 = f32[512,8]{0,1:T(8,128)S(1)} all-reduce(f32[512,8]{0,1:T(8,128)S(1)} %fusion.24), channel_id=1, replica_groups=mesh['groups'=2,'seq'=4,'head'=2,'rep'=2] {'seq'}, use_global_device_ids=true, to_apply=%region_5.0 | all-reduce | flops 4096 | bytes 32768 | tf_op jit(solution)/shard_map/psum | solution.py:113
  107.7 25.8 %all-reduce.2.cloned.1.call-done = f32[512,512]{0,1:T(8,128)} async-done(((f32[512,512]{0,1:T(8,128)}), f32[512,512]{0,1:T(8,128)}) %all-reduce.2.cloned.1.call-update) | async-done | bytes 1048592 | tf_op jit(solution)/shard_map/psum | solution.py:113
  133.5 2.2 fusion.42
  135.7 0.0 all-gather.2.cloned.1.call-update
  135.7 3.0 %copy.20 = bf16[2,1024,512]{1,2,0:T(8,128)(2,1)S(1)} copy(bf16[2,1024,512]{2,1,0:T(8,128)(2,1)} %param.9) | data formatting | bytes 4194304 | tf_op args[1]
  138.7 1.2 fusion.47
  139.9 1.3 collective-permute-start.1
  141.2 5.5 %collective-permute-start = (bf16[2,512,512]{1,2,0:T(8,128)(2,1)S(1)}, bf16[2,512,512]{1,2,0:T(8,128)(2,1)}, u32[]{:S(2)}, u32[]{:S(2)}) collective-permute-start(bf16[2,512,512]{1,2,0:T(8,128)(2,1)S(1)} %get-tuple-element.181), channel_id=1, source_target_pairs={{0,4},{4,8},{8,12},{1,5},{5,9},{9,13},{2,6},{6,10},{10,14},{3,7},{... | collective-permute-start | bytes 3145736 | tf_op jit(solution)/shard_map/ppermute | solution.py:20
  146.7 20.5 %collective-permute-done.1 = bf16[2,512,512]{1,2,0:T(8,128)(2,1)} collective-permute-done((bf16[2,512,512]{1,2,0:T(8,128)(2,1)}, bf16[2,512,512]{1,2,0:T(8,128)(2,1)}, u32[]{:S(2)}, u32[]{:S(2)}) %collective-permute-start.1) | collective-permute-done | bytes 1048608 | tf_op jit(solution)/shard_map/ppermute | solution.py:22
  167.2 0.9 collective-permute-done
  168.1 3.4 %pad_maximum_fusion = bf16[2,2048,512]{1,2,0:T(8,128)(2,1)} fusion(bf16[2,512,512]{1,2,0:T(8,128)(2,1)} %collective-permute-done.1, bf16[2,1024,512]{1,2,0:T(8,128)(2,1)S(1)} %copy.20, bf16[2,512,512]{1,2,0:T(8,128)(2,1)} %collective-permute-done), kind=kLoop, calls=%fused_computation.35 | loop fusion | flops 12582912 | bytes 8388608 | tf_op jit(solution)/shard_map/concatenate | solution.py:18
  171.5 0.0 all-gather.2.cloned.1.call-done
  171.5 3.5 %fusion.36 = bf16[512,512]{0,1:T(8,128)(2,1)S(1)} fusion(bf16[512,2048]{0,1:T(8,128)(2,1)} %all-gather.2.cloned.1.call-done, bf16[2,2048,512]{2,1,0:T(8,128)(2,1)} %param.13), kind=kOutput, calls=%fused_computation.45 | convolution fusion | flops 1074003968 | bytes 4718592 | tf_op jit(solution)/shard_map/dot_general | solution.py:116
  175.0 4.3 %fusion.39 = bf16[512,512]{0,1:T(8,128)(2,1)} fusion(bf16[512,2048]{0,1:T(8,128)(2,1)} %all-gather.2.cloned.1.call-done, bf16[2,2048,512]{2,1,0:T(8,128)(2,1)} %param.13), kind=kOutput, calls=%fused_computation.46 | convolution fusion | flops 1074003968 | bytes 4718592 | tf_op jit(solution)/shard_map/dot_general | solution.py:117
  179.3 0.0 copy-done
  179.3 98.0 %while.12 = (s32[]{:T(128)}, bf16[2,512,512]{2,1,0:T(8,128)(2,1)}, s32[2]{0:T(128)S(1)}, bf16[1024,512]{1,0:T(8,128)(2,1)}, bf16[512,8,64]{0,2,1:T(8,128)(2,1)S(...) while((s32[]{:T(128)}, bf16[2,512,512]{2,1,0:T(8,128)(2,1)}, ...), condition=%wide.region_11.12_spmd, body=%wide.region_6.11_spmd.sunk | while | flops 2225596416 | bytes 137660848 | solution.py:148
  179.5 0.7 dynamic_slice.33
  180.9 3.3 %constant_dynamic-slice_fusion.8 = (bf16[1,1536,512]{1,2,0:T(8,128)(2,1)}, bf16[1,1536,512]{1,2,0:T(8,128)(2,1)S(1)}) fusion(bf16[2,2048,512]{1,2,0:T(8,128)(2,1)} %get-tuple-element.310, s32[]{:T(128)S(6)} %select_n.24, s32[]{:T(128)S(6)} %add.106), kind=kLoop, calls=%fused_computation.22.clone.1 | loop fusion | bytes 6291464 | tf_op jit(solution)/shard_map/while/body/eval_jaxpr/slice | solution.py:132
  184.2 1.1 constant_dynamic-slice_fusion.9
  185.3 0.2 copy.31
  185.5 0.7 compare_and_fusion.2
  186.3 0.5 subtract_abs_fusion.2
  186.7 14.5 %fusion.83 = (f32[8,512]{1,0:T(8,128)S(1)}, f32[8,512,1536]{2,1,0:T(8,128)}) fusion(bf16[512,8,64]{0,2,1:T(8,128)(2,1)S(1)} %bitcast.95, bf16[1536,8,64]{0,2,1:T(8,128)(2,1)} %bitcast.97, pred[512,1536]{1,0:T(8,128)(4,1)S(1)} %compare_and_fusion.2, s32[8]{0:T(128)S(1)} %get-tuple-element.308, s32[512,1536]{1,0:T(8,128)S(1)} %subtract_abs_fusion.2), kind=kOutput, calls=%fused_computation.53.clone.1 | convolution fusion | flops 836759552 | bytes 31211552 | tf_op jit(solution)/shard_map/while/body/eval_jaxpr/qhd,khd->hqk/dot_general | solution.py:54
  201.2 1.3 multiply_reduce_fusion.2
  202.5 10.3 %fusion.84 = f32[512,8,64]{0,2,1:T(8,128)S(1)} fusion(bf16[1536,8,64]{0,2,1:T(8,128)(2,1)S(1)} %bitcast.94, f32[8,512,1536]{2,1,0:T(8,128)} %get-tuple-element.264, f32[8,512]{1,0:T(8,128)S(1)} %max.13), kind=kOutput, calls=%fused_computation.16.clone.1 | convolution fusion | flops 817889280 | bytes 27803648 | tf_op jit(solution)/shard_map/while/body/eval_jaxpr/hqk,khd->qhd/dot_general | solution.py:73
  212.8 1.4 fusion.85
  214.2 11.3 %fusion.86 = f32[8,512]{1,0:T(8,128)S(1)} fusion(f32[8,512,1536]{2,1,0:T(8,128)} %get-tuple-element.264, f32[8,512]{1,0:T(8,128)S(1)} %max.13), kind=kLoop, calls=%fused_computation.2.clone.1 | loop fusion | flops 12578816 | bytes 25198592 | tf_op jit(solution)/shard_map/while/body/eval_jaxpr/reduce_sum | solution.py:66
  225.5 0.0 copy-start.1
  225.6 1.6 divide_convert_fusion.2
  227.2 0.2 copy.32
  227.5 0.0 copy-start.2
  227.5 1.0 copy-done.2
  228.4 0.7 dynamic_slice.33
  229.8 3.3 %constant_dynamic-slice_fusion.8 = (bf16[1,1536,512]{1,2,0:T(8,128)(2,1)}, bf16[1,1536,512]{1,2,0:T(8,128)(2,1)S(1)}) fusion(bf16[2,2048,512]{1,2,0:T(8,128)(2,1)} %get-tuple-element.310, s32[]{:T(128)S(6)} %select_n.24, s32[]{:T(128)S(6)} %add.106), kind=kLoop, calls=%fused_computation.22.clone.1 | loop fusion | bytes 6291464 | tf_op jit(solution)/shard_map/while/body/eval_jaxpr/slice | solution.py:132
  233.1 1.1 constant_dynamic-slice_fusion.9
  234.2 0.2 copy.31
  234.4 0.7 compare_and_fusion.2
  235.1 0.5 subtract_abs_fusion.2
  235.6 14.5 %fusion.83 = (f32[8,512]{1,0:T(8,128)S(1)}, f32[8,512,1536]{2,1,0:T(8,128)}) fusion(bf16[512,8,64]{0,2,1:T(8,128)(2,1)S(1)} %bitcast.95, bf16[1536,8,64]{0,2,1:T(8,128)(2,1)} %bitcast.97, pred[512,1536]{1,0:T(8,128)(4,1)S(1)} %compare_and_fusion.2, s32[8]{0:T(128)S(1)} %get-tuple-element.308, s32[512,1536]{1,0:T(8,128)S(1)} %subtract_abs_fusion.2), kind=kOutput, calls=%fused_computation.53.clone.1 | convolution fusion | flops 836759552 | bytes 31211552 | tf_op jit(solution)/shard_map/while/body/eval_jaxpr/qhd,khd->hqk/dot_general | solution.py:54
  250.1 1.3 multiply_reduce_fusion.2
  251.4 10.3 %fusion.84 = f32[512,8,64]{0,2,1:T(8,128)S(1)} fusion(bf16[1536,8,64]{0,2,1:T(8,128)(2,1)S(1)} %bitcast.94, f32[8,512,1536]{2,1,0:T(8,128)} %get-tuple-element.264, f32[8,512]{1,0:T(8,128)S(1)} %max.13), kind=kOutput, calls=%fused_computation.16.clone.1 | convolution fusion | flops 817889280 | bytes 27803648 | tf_op jit(solution)/shard_map/while/body/eval_jaxpr/hqk,khd->qhd/dot_general | solution.py:73
  261.7 1.4 fusion.85
  263.1 11.3 %fusion.86 = f32[8,512]{1,0:T(8,128)S(1)} fusion(f32[8,512,1536]{2,1,0:T(8,128)} %get-tuple-element.264, f32[8,512]{1,0:T(8,128)S(1)} %max.13), kind=kLoop, calls=%fused_computation.2.clone.1 | loop fusion | flops 12578816 | bytes 25198592 | tf_op jit(solution)/shard_map/while/body/eval_jaxpr/reduce_sum | solution.py:66
  274.4 0.0 copy-start.1
  274.5 1.6 divide_convert_fusion.2
  276.1 0.2 copy.32
  276.3 0.0 copy-start.2
  276.4 1.0 copy-done.2
  (26 shorter events, 0.2 us)
Async XLA Ops:
  6.5 28.0 %reduce-scatter.2.cloned.1.call-start = ((), (), s32[]{:S(2)}) async-start(), calls=%async_computation.1 | async-start | bytes 655360 | tf_op jit(solution)/shard_map/reduce_scatter | solution.py:92
  10.0 123.5 %all-reduce.2.cloned.1.call-start = ((), (), s32[]{:S(2)}) async-start(), calls=%async_computation.2 | async-start | bytes 2097152 | tf_op jit(solution)/shard_map/psum | solution.py:113
  83.0 88.5 %all-gather.2.cloned.1.call-start = ((), (), s32[]{:S(2)}) async-start(), calls=%async_computation.3 | async-start | bytes 2621440 | tf_op jit(solution)/shard_map/all_gather | solution.py:115
  139.9 27.3 %collective-permute-start.1 = (bf16[2,512,512]{1,2,0:T(8,128)(2,1)}, bf16[2,512,512]{1,2,0:T(8,128)(2,1)}, u32[]{:S(2)}, u32[]{:S(2)}) collective-permute-start(bf16[2,512,512]{1,2,0:T(8,128)(2,1)} %get-tuple-element.182), channel_id=1, source_target_pairs={{4,0},{8,4},{12,8},{5,1},{9,5},{13,9},{6,2},{10,6},{14,10},{7,3},{... | collective-permute-start | bytes 3145736 | tf_op jit(solution)/shard_map/ppermute | solution.py:22
  141.2 26.9 %collective-permute-start = (bf16[2,512,512]{1,2,0:T(8,128)(2,1)S(1)}, bf16[2,512,512]{1,2,0:T(8,128)(2,1)}, u32[]{:S(2)}, u32[]{:S(2)}) collective-permute-start(bf16[2,512,512]{1,2,0:T(8,128)(2,1)S(1)} %get-tuple-element.181), channel_id=1, source_target_pairs={{0,4},{4,8},{8,12},{1,5},{5,9},{9,13},{2,6},{6,10},{10,14},{3,7},{... | collective-permute-start | bytes 3145736 | tf_op jit(solution)/shard_map/ppermute | solution.py:20
  171.5 7.9 %copy-start = (s32[2,1024]{1,0:T(2,128)S(1)}, s32[2,1024]{1,0:T(2,128)}, u32[]{:S(2)}) copy-start(s32[2,1024]{1,0:T(2,128)} %param.11) | copy-start | bytes 24580
  171.5 7.9 %copy-start.3 = (s32[8]{0:T(128)S(1)}, s32[8]{0:T(128)}, u32[]{:S(2)}) copy-start(s32[8]{0:T(128)} %param.12) | copy-start | bytes 100
  214.2 11.4 %copy-start.4 = (bf16[512,8,64]{0,2,1:T(8,128)(2,1)S(1)}, bf16[512,8,64]{0,2,1:T(8,128)(2,1)}, u32[]{:S(2)}) copy-start(bf16[512,8,64]{0,2,1:T(8,128)(2,1)} %get-tuple-element.311) | copy-start | bytes 1572868 | tf_op jit(solution)/shard_map/while
  225.5 1.9 copy-start.1
  227.5 1.0 copy-start.2
  263.1 11.4 %copy-start.4 = (bf16[512,8,64]{0,2,1:T(8,128)(2,1)S(1)}, bf16[512,8,64]{0,2,1:T(8,128)(2,1)}, u32[]{:S(2)}) copy-start(bf16[512,8,64]{0,2,1:T(8,128)(2,1)} %get-tuple-element.311) | copy-start | bytes 1572868 | tf_op jit(solution)/shard_map/while
  274.4 1.9 copy-start.1
  276.3 1.0 copy-start.2
Sparse Core Ops, SparseCore 0:
  10.1 24.3 reduce-scatter.1
  83.1 50.3 all-reduce.1
  135.8 21.9 all-gather.1
where the time goes:
time: 285 us; the launch traced here: 284 us
  matrix products  82.2 us (29%)
  waiting for transfers between devices  68.9 us (24%)
  blocking collectives  49 us (17%)
  other arithmetic  41.6 us (15%)
  local copies, waits for them, and re-layouts  20.1 us (7%)
  between operations  13.2 us (5%)
  starting transfers between devices  6.9 us (2%)
    dot_general x2, matrix products, attend(): jnp.einsum('qhd,khd->hqk', query_block, window_keys, preferred_element_ty...  28.9 us
    psum x1, waiting for transfers between devices, shards(): whole_sum, whole_total = lax.psum((row_sum, row_total), 'seq')  25.8 us
    reduce_sum x4, other arithmetic, attend(): totals = jnp.sum(pack_weights, axis=2) + jnp.sum(window_weights, axis=2)  25.4 us
    reduce_scatter x1, waiting for transfers between devices, shards(): lax.psum_scatter(picked.astype(jnp.bfloat16), 'seq', scatter_dimension=0,...  21.7 us
    dot_general x2, matrix products, attend(): jnp.einsum('hqk,khd->qhd', window_weights.astype(jnp.bfloat16), window_va...  20.6 us
    ppermute x1, waiting for transfers between devices, padded(): lax.ppermute(head, axis, [((i + 1) % count, i) for i in range(ends)])  20.5 us
    psum x1, blocking collectives, shards(): whole_sum, whole_total = lax.psum((row_sum, row_total), 'seq')  17 us
    all_gather x1, blocking collectives, shards(): pack_query = lax.all_gather(picked_share, 'seq', axis=0, tiled=True)  16.1 us
  transfers between devices with their start and end apart: 5, of which 4 were waited for; matrix products, arithmetic and copies ran while one was open for 6% of the time, Pallas kernels for 0%

commit v1 on v0

--- a/solution.py
+++ b/solution.py
@@ -92,7 +92,12 @@
     picked_share = lax.psum_scatter(
         picked.astype(jnp.bfloat16), "seq", scatter_dimension=0, tiled=True
     )
-    pack_query = lax.all_gather(picked_share, "seq", axis=0, tiled=True)
+    ring = [picked_share]
+    for hop in range(3):
+        ring.append(lax.ppermute(ring[-1], "seq", [(dev, (dev + 1) % 4) for dev in range(4)]))
+    pack_query = jnp.roll(
+        jnp.concatenate(ring[::-1], axis=0), (lax.axis_index("seq") + 1) * ring[0].shape[0], axis=0
+    )
     query_heads = pack_query.reshape(PACK, heads_here, HEAD_DIM)
     key_heads = keys_values[0].reshape(tokens_here, heads_here, HEAD_DIM)
     value_heads = keys_values[1].reshape(tokens_here, heads_here, HEAD_DIM)

time: 285 us -> 291 us (1.021)
  waiting for transfers between devices: 68.9 us -> 89.4 us
  blocking collectives: 49 us -> 32.9 us
    ppermute x0 -> x3, waiting for transfers between devices: none -> 17.8 us  [shards(): lax.ppermute(ring[-1], 'seq', [(dev, (dev + 1) % 4) for dev in range(4)])]
    all_gather x1 -> x0, blocking collectives: 16.1 us -> none  [shards(): pack_query = lax.all_gather(picked_share, 'seq', axis=0, tiled=True)]
  transfers between devices with their start and end apart: 5 -> 8, of which waited for: 4 -> 7; matrix products, arithmetic and copies ran while one was open for 6% -> 6% of each run, Pallas kernels for 0% -> 0%
where the time goes in v1:
time: 291 us; the launch traced here: 290 us
  waiting for transfers between devices  89.4 us (31%)
  matrix products  82.2 us (28%)
  other arithmetic  41.7 us (14%)
  blocking collectives  32.9 us (11%)
  local copies, waits for them, and re-layouts  22.1 us (8%)
  between operations  13.3 us (5%)
  starting transfers between devices  6.91 us (2%)
    dot_general x2, matrix products, attend(): jnp.einsum('qhd,khd->hqk', query_block, window_keys, preferred_element_ty...  28.9 us
    psum x1, waiting for transfers between devices, shards(): whole_sum, whole_total = lax.psum((row_sum, row_total), 'seq')  25.7 us
    reduce_sum x4, other arithmetic, attend(): totals = jnp.sum(pack_weights, axis=2) + jnp.sum(window_weights, axis=2)  25.4 us
    reduce_scatter x1, waiting for transfers between devices, shards(): lax.psum_scatter(picked.astype(jnp.bfloat16), 'seq', scatter_dimension=0,...  24.4 us
    dot_general x2, matrix products, attend(): jnp.einsum('hqk,khd->qhd', window_weights.astype(jnp.bfloat16), window_va...  20.6 us
    ppermute x1, waiting for transfers between devices, padded(): lax.ppermute(head, axis, [((i + 1) % count, i) for i in range(ends)])  20.5 us
    ppermute x3, waiting for transfers between devices, shards(): lax.ppermute(ring[-1], 'seq', [(dev, (dev + 1) % 4) for dev in range(4)])  17.8 us
    psum x1, blocking collectives, shards(): whole_sum, whole_total = lax.psum((row_sum, row_total), 'seq')  17.3 us
  transfers between devices with their start and end apart: 8, of which 7 were waited for; matrix products, arithmetic and copies ran while one was open for 6% of the time, Pallas kernels for 0%

profile of v1, /device:TPU:0, one launch (start us, length us, event | category | flops | bytes accessed | tf_op | source)
XLA Modules:
  0.0 290.4 jit_solution(16665431352732465218)
XLA Ops:
  6.5 0.7 broadcast_subtract_fusion
  7.2 2.8 fusion.35
  10.0 0.0 reduce-scatter.2.cloned.1.call-update
  10.0 0.0 all-reduce.2.cloned.1.call-start
  10.1 24.4 %reduce-scatter.2.cloned.1.call-done = bf16[128,512]{1,0:T(8,128)(2,1)} async-done(((bf16[512,512]{1,0:T(8,128)(2,1)}), bf16[128,512]{1,0:T(8,128)(2,1)}) %reduce-scatter.2.cloned.1.call-update) | async-done | bytes 131088 | tf_op jit(solution)/shard_map/reduce_scatter | solution.py:92
  34.5 7.0 %collective-permute-done = bf16[128,512]{1,0:T(8,128)(2,1)S(1)} collective-permute-done((bf16[128,512]{1,0:T(8,128)(2,1)}, bf16[128,512]{1,0:T(8,128)(2,1)S(1)}, u32[]{:S(2)}, u32[]{:S(2)}) %collective-permute-start) | collective-permute-done | bytes 131104 | tf_op jit(solution)/shard_map/ppermute | solution.py:97
  41.5 6.8 %collective-permute-done.1 = bf16[128,512]{1,0:T(8,128)(2,1)S(1)} collective-permute-done((bf16[128,512]{1,0:T(8,128)(2,1)S(1)}, bf16[128,512]{1,0:T(8,128)(2,1)S(1)}, u32[]{:S(2)}, u32[]{:S(2)}) %collective-permute-start.1) | collective-permute-done | bytes 131104 | tf_op jit(solution)/shard_map/ppermute | solution.py:97
  48.3 1.7 fusion.48
  50.0 0.5 copy.18
  50.5 0.5 copy.17
  51.1 4.1 %collective-permute-done.2 = bf16[128,512]{1,0:T(8,128)(2,1)} collective-permute-done((bf16[128,512]{1,0:T(8,128)(2,1)S(1)}, bf16[128,512]{1,0:T(8,128)(2,1)}, u32[]{:S(2)}, u32[]{:S(2)}) %collective-permute-start.2) | collective-permute-done | bytes 131104 | tf_op jit(solution)/shard_map/ppermute | solution.py:97
  55.1 0.9 constant_dynamic-update-slice_fusion.8
  56.1 0.9 constant_dynamic-update-slice_fusion.4
  57.1 0.2 copy.16
  57.4 8.1 %bitcast_reduce_fusion = (f32[512,8]{0,1:T(8,128)S(1)}, f32[8,512,1024]{2,1,0:T(8,128)}) fusion(bf16[512,8,64]{0,2,1:T(8,128)(2,1)S(1)} %bitcast.103, bf16[1024,8,64]{0,2,1:T(8,128)(2,1)S(1)} %bitcast.101), kind=kOutput, calls=%fused_computation.30 | convolution fusion | flops 545255424 | bytes 18366464 | tf_op jit(solution)/shard_map/phd,thd->pht/dot_general | solution.py:105
  65.5 15.5 %pmax.7 = f32[512,8]{0,1:T(8,128)S(1)} all-reduce(f32[512,8]{0,1:T(8,128)S(1)} %get-tuple-element.185), channel_id=1, replica_groups=mesh['groups'=2,'seq'=4,'head'=2,'rep'=2] {'seq'}, use_global_device_ids=true, to_apply=%region_2.3 | all-reduce | flops 4096 | bytes 32768 | tf_op jit(solution)/shard_map/pmax | solution.py:109
  81.0 8.2 %fusion.26 = f32[8,512,64]{1,2,0:T(8,128)} fusion(bf16[1024,8,64]{0,2,1:T(8,128)(2,1)S(1)} %bitcast.100, f32[8,512,1024]{2,1,0:T(8,128)} %get-tuple-element.186, f32[512,8]{0,1:T(8,128)S(1)} %pmax.7), kind=kOutput, calls=%fused_computation.34 | convolution fusion | flops 549453824 | bytes 18890752 | tf_op jit(solution)/shard_map/pht,thd->phd/dot_general | solution.py:112
  89.1 0.0 all-reduce.2.cloned.1.call-update
  89.2 0.0 all-gather.2.cloned.1.call-start
  89.2 7.7 %fusion.24 = f32[512,8]{0,1:T(8,128)S(1)} fusion(f32[8,512,1024]{2,1,0:T(8,128)} %get-tuple-element.186, f32[512,8]{0,1:T(8,128)S(1)} %pmax.7), kind=kLoop, calls=%fused_computation.32 | loop fusion | flops 12578816 | bytes 16809984 | tf_op jit(solution)/shard_map/reduce_sum | solution.py:111
  97.0 17.3 %psum.15 = f32[512,8]{0,1:T(8,128)S(1)} all-reduce(f32[512,8]{0,1:T(8,128)S(1)} %fusion.24), channel_id=1, replica_groups=mesh['groups'=2,'seq'=4,'head'=2,'rep'=2] {'seq'}, use_global_device_ids=true, to_apply=%region_5.6 | all-reduce | flops 4096 | bytes 32768 | tf_op jit(solution)/shard_map/psum | solution.py:118
  114.3 25.7 %all-reduce.2.cloned.1.call-done = f32[512,512]{0,1:T(8,128)} async-done(((f32[512,512]{0,1:T(8,128)}), f32[512,512]{0,1:T(8,128)}) %all-reduce.2.cloned.1.call-update) | async-done | bytes 1048592 | tf_op jit(solution)/shard_map/psum | solution.py:118
  140.0 2.2 fusion.42
  142.2 0.0 all-gather.2.cloned.1.call-update
  142.2 3.0 %copy.19 = bf16[2,1024,512]{1,2,0:T(8,128)(2,1)S(1)} copy(bf16[2,1024,512]{2,1,0:T(8,128)(2,1)} %param.9) | data formatting | bytes 4194304 | tf_op args[1]
  145.2 1.2 fusion.47
  146.4 1.3 collective-permute-start.4
  147.7 5.5 %collective-permute-start.3 = (bf16[2,512,512]{1,2,0:T(8,128)(2,1)S(1)}, bf16[2,512,512]{1,2,0:T(8,128)(2,1)}, u32[]{:S(2)}, u32[]{:S(2)}) collective-permute-start(bf16[2,512,512]{1,2,0:T(8,128)(2,1)S(1)} %get-tuple-element.181), channel_id=1, source_target_pairs={{0,4},{4,8},{8,12},{1,5},{5,9},{9,13},{2,6},{6,10},{10,14},{3,7},{... | collective-permute-start | bytes 3145736 | tf_op jit(solution)/shard_map/ppermute | solution.py:20
  153.2 20.5 %collective-permute-done.4 = bf16[2,512,512]{1,2,0:T(8,128)(2,1)} collective-permute-done((bf16[2,512,512]{1,2,0:T(8,128)(2,1)}, bf16[2,512,512]{1,2,0:T(8,128)(2,1)}, u32[]{:S(2)}, u32[]{:S(2)}) %collective-permute-start.4) | collective-permute-done | bytes 1048608 | tf_op jit(solution)/shard_map/ppermute | solution.py:22
  173.7 0.9 collective-permute-done.3
  174.6 3.4 %pad_maximum_fusion = bf16[2,2048,512]{1,2,0:T(8,128)(2,1)} fusion(bf16[2,512,512]{1,2,0:T(8,128)(2,1)} %collective-permute-done.4, bf16[2,1024,512]{1,2,0:T(8,128)(2,1)S(1)} %copy.19, bf16[2,512,512]{1,2,0:T(8,128)(2,1)} %collective-permute-done.3), kind=kLoop, calls=%fused_computation.35 | loop fusion | flops 12582912 | bytes 8388608 | tf_op jit(solution)/shard_map/concatenate | solution.py:18
  178.0 0.0 all-gather.2.cloned.1.call-done
  178.0 3.5 %fusion.36 = bf16[512,512]{0,1:T(8,128)(2,1)S(1)} fusion(bf16[512,2048]{0,1:T(8,128)(2,1)} %all-gather.2.cloned.1.call-done, bf16[2,2048,512]{2,1,0:T(8,128)(2,1)} %param.13), kind=kOutput, calls=%fused_computation.45 | convolution fusion | flops 1074003968 | bytes 4718592 | tf_op jit(solution)/shard_map/dot_general | solution.py:121
  181.5 4.3 %fusion.39 = bf16[512,512]{0,1:T(8,128)(2,1)} fusion(bf16[512,2048]{0,1:T(8,128)(2,1)} %all-gather.2.cloned.1.call-done, bf16[2,2048,512]{2,1,0:T(8,128)(2,1)} %param.13), kind=kOutput, calls=%fused_computation.46 | convolution fusion | flops 1074003968 | bytes 4718592 | tf_op jit(solution)/shard_map/dot_general | solution.py:122
  185.9 98.0 %while.12 = (s32[]{:T(128)}, bf16[2,512,512]{2,1,0:T(8,128)(2,1)}, s32[2]{0:T(128)S(1)}, bf16[1024,512]{1,0:T(8,128)(2,1)}, bf16[512,8,64]{0,2,1:T(8,128)(2,1)S(...) while((s32[]{:T(128)}, bf16[2,512,512]{2,1,0:T(8,128)(2,1)}, ...), condition=%wide.region_11.12_spmd, body=%wide.region_6.11_spmd.sunk | while | flops 2225596416 | bytes 137660848 | solution.py:153
  186.1 0.7 dynamic_slice.39
  187.4 3.3 %constant_dynamic-slice_fusion.9 = (bf16[1,1536,512]{1,2,0:T(8,128)(2,1)}, bf16[1,1536,512]{1,2,0:T(8,128)(2,1)S(1)}) fusion(bf16[2,2048,512]{1,2,0:T(8,128)(2,1)} %get-tuple-element.310, s32[]{:T(128)S(6)} %select_n.39, s32[]{:T(128)S(6)} %add.122), kind=kLoop, calls=%fused_computation.22.clone.1 | loop fusion | bytes 6291464 | tf_op jit(solution)/shard_map/while/body/eval_jaxpr/slice | solution.py:137
  190.7 1.1 constant_dynamic-slice_fusion.10
  191.8 0.2 copy.30
  192.1 0.7 compare_and_fusion.2
  192.8 0.5 subtract_abs_fusion.2
  193.3 14.5 %fusion.83 = (f32[8,512]{1,0:T(8,128)S(1)}, f32[8,512,1536]{2,1,0:T(8,128)}) fusion(bf16[512,8,64]{0,2,1:T(8,128)(2,1)S(1)} %bitcast.95, bf16[1536,8,64]{0,2,1:T(8,128)(2,1)} %bitcast.97, pred[512,1536]{1,0:T(8,128)(4,1)S(1)} %compare_and_fusion.2, s32[8]{0:T(128)S(1)} %get-tuple-element.308, s32[512,1536]{1,0:T(8,128)S(1)} %subtract_abs_fusion.2), kind=kOutput, calls=%fused_computation.62.clone.1 | convolution fusion | flops 836759552 | bytes 31211552 | tf_op jit(solution)/shard_map/while/body/eval_jaxpr/qhd,khd->hqk/dot_general | solution.py:54
  207.7 1.3 multiply_reduce_fusion.2
  209.0 10.3 %fusion.84 = f32[512,8,64]{0,2,1:T(8,128)S(1)} fusion(bf16[1536,8,64]{0,2,1:T(8,128)(2,1)S(1)} %bitcast.94, f32[8,512,1536]{2,1,0:T(8,128)} %get-tuple-element.264, f32[8,512]{1,0:T(8,128)S(1)} %max.13), kind=kOutput, calls=%fused_computation.16.clone.1 | convolution fusion | flops 817889280 | bytes 27803648 | tf_op jit(solution)/shard_map/while/body/eval_jaxpr/hqk,khd->qhd/dot_general | solution.py:73
  219.3 1.4 fusion.85
  220.7 11.3 %fusion.86 = f32[8,512]{1,0:T(8,128)S(1)} fusion(f32[8,512,1536]{2,1,0:T(8,128)} %get-tuple-element.264, f32[8,512]{1,0:T(8,128)S(1)} %max.13), kind=kLoop, calls=%fused_computation.2.clone.1 | loop fusion | flops 12578816 | bytes 25198592 | tf_op jit(solution)/shard_map/while/body/eval_jaxpr/reduce_sum | solution.py:66
  232.1 1.6 divide_convert_fusion.2
  233.7 0.2 copy.31
  234.0 0.0 copy-start.3
  234.0 1.0 copy-done.3
  234.9 0.7 dynamic_slice.39
  236.3 3.3 %constant_dynamic-slice_fusion.9 = (bf16[1,1536,512]{1,2,0:T(8,128)(2,1)}, bf16[1,1536,512]{1,2,0:T(8,128)(2,1)S(1)}) fusion(bf16[2,2048,512]{1,2,0:T(8,128)(2,1)} %get-tuple-element.310, s32[]{:T(128)S(6)} %select_n.39, s32[]{:T(128)S(6)} %add.122), kind=kLoop, calls=%fused_computation.22.clone.1 | loop fusion | bytes 6291464 | tf_op jit(solution)/shard_map/while/body/eval_jaxpr/slice | solution.py:137
  239.6 1.1 constant_dynamic-slice_fusion.10
  240.7 0.2 copy.30
  240.9 0.7 compare_and_fusion.2
  241.7 0.5 subtract_abs_fusion.2
  242.1 14.5 %fusion.83 = (f32[8,512]{1,0:T(8,128)S(1)}, f32[8,512,1536]{2,1,0:T(8,128)}) fusion(bf16[512,8,64]{0,2,1:T(8,128)(2,1)S(1)} %bitcast.95, bf16[1536,8,64]{0,2,1:T(8,128)(2,1)} %bitcast.97, pred[512,1536]{1,0:T(8,128)(4,1)S(1)} %compare_and_fusion.2, s32[8]{0:T(128)S(1)} %get-tuple-element.308, s32[512,1536]{1,0:T(8,128)S(1)} %subtract_abs_fusion.2), kind=kOutput, calls=%fused_computation.62.clone.1 | convolution fusion | flops 836759552 | bytes 31211552 | tf_op jit(solution)/shard_map/while/body/eval_jaxpr/qhd,khd->hqk/dot_general | solution.py:54
  256.6 1.3 multiply_reduce_fusion.2
  257.9 10.3 %fusion.84 = f32[512,8,64]{0,2,1:T(8,128)S(1)} fusion(bf16[1536,8,64]{0,2,1:T(8,128)(2,1)S(1)} %bitcast.94, f32[8,512,1536]{2,1,0:T(8,128)} %get-tuple-element.264, f32[8,512]{1,0:T(8,128)S(1)} %max.13), kind=kOutput, calls=%fused_computation.16.clone.1 | convolution fusion | flops 817889280 | bytes 27803648 | tf_op jit(solution)/shard_map/while/body/eval_jaxpr/hqk,khd->qhd/dot_general | solution.py:73
  268.2 1.4 fusion.85
  269.6 11.3 %fusion.86 = f32[8,512]{1,0:T(8,128)S(1)} fusion(f32[8,512,1536]{2,1,0:T(8,128)} %get-tuple-element.264, f32[8,512]{1,0:T(8,128)S(1)} %max.13), kind=kLoop, calls=%fused_computation.2.clone.1 | loop fusion | flops 12578816 | bytes 25198592 | tf_op jit(solution)/shard_map/while/body/eval_jaxpr/reduce_sum | solution.py:66
  281.0 1.6 divide_convert_fusion.2
  282.6 0.2 copy.31
  282.9 1.0 copy-done.3
  (42 shorter events, 0.3 us)
Async XLA Ops:
  6.5 28.0 %reduce-scatter.2.cloned.1.call-start = ((), (), s32[]{:S(2)}) async-start(), calls=%async_computation.1 | async-start | bytes 655360 | tf_op jit(solution)/shard_map/reduce_scatter | solution.py:92
  10.0 130.0 %all-reduce.2.cloned.1.call-start = ((), (), s32[]{:S(2)}) async-start(), calls=%async_computation.2 | async-start | bytes 2097152 | tf_op jit(solution)/shard_map/psum | solution.py:118
  34.5 21.6 %copy-start = (bf16[128,512]{1,0:T(8,128)(2,1)S(1)}, bf16[128,512]{1,0:T(8,128)(2,1)}, u32[]{:S(2)}) copy-start(bf16[128,512]{1,0:T(8,128)(2,1)} %reduce-scatter.2.cloned.1.call-done) | copy-start | bytes 393220
  34.5 7.0 %collective-permute-start = (bf16[128,512]{1,0:T(8,128)(2,1)}, bf16[128,512]{1,0:T(8,128)(2,1)S(1)}, u32[]{:S(2)}, u32[]{:S(2)}) collective-permute-start(bf16[128,512]{1,0:T(8,128)(2,1)} %reduce-scatter.2.cloned.1.call-done), channel_id=1, source_target_pairs={{0,4},{4,8},{8,12},{12,0},{1,5},{5,9},{9,13},{13,1},{2,6},{6,10},{... | collective-permute-start | bytes 393224 | tf_op jit(solution)/shard_map/ppermute | solution.py:97
  41.5 6.8 %collective-permute-start.1 = (bf16[128,512]{1,0:T(8,128)(2,1)S(1)}, bf16[128,512]{1,0:T(8,128)(2,1)S(1)}, u32[]{:S(2)}, u32[]{:S(2)}) collective-permute-start(bf16[128,512]{1,0:T(8,128)(2,1)S(1)} %collective-permute-done), channel_id=1, source_target_pairs={{0,4},{4,8},{8,12},{12,0},{1,5},{5,9},{9,13},{13,1},{2,6},{6,10},{... | collective-permute-start | bytes 393224 | tf_op jit(solution)/shard_map/ppermute | solution.py:97
  48.3 6.9 %collective-permute-start.2 = (bf16[128,512]{1,0:T(8,128)(2,1)S(1)}, bf16[128,512]{1,0:T(8,128)(2,1)}, u32[]{:S(2)}, u32[]{:S(2)}) collective-permute-start(bf16[128,512]{1,0:T(8,128)(2,1)S(1)} %collective-permute-done.1), channel_id=1, source_target_pairs={{0,4},{4,8},{8,12},{12,0},{1,5},{5,9},{9,13},{13,1},{2,6},{6,10},{... | collective-permute-start | bytes 393224 | tf_op jit(solution)/shard_map/ppermute | solution.py:97
  89.2 88.8 %all-gather.2.cloned.1.call-start = ((), (), s32[]{:S(2)}) async-start(), calls=%async_computation.3 | async-start | bytes 2621440 | tf_op jit(solution)/shard_map/all_gather | solution.py:120
  146.4 27.3 %collective-permute-start.4 = (bf16[2,512,512]{1,2,0:T(8,128)(2,1)}, bf16[2,512,512]{1,2,0:T(8,128)(2,1)}, u32[]{:S(2)}, u32[]{:S(2)}) collective-permute-start(bf16[2,512,512]{1,2,0:T(8,128)(2,1)} %get-tuple-element.182), channel_id=1, source_target_pairs={{4,0},{8,4},{12,8},{5,1},{9,5},{13,9},{6,2},{10,6},{14,10},{7,3},{... | collective-permute-start | bytes 3145736 | tf_op jit(solution)/shard_map/ppermute | solution.py:22
  147.7 26.9 %collective-permute-start.3 = (bf16[2,512,512]{1,2,0:T(8,128)(2,1)S(1)}, bf16[2,512,512]{1,2,0:T(8,128)(2,1)}, u32[]{:S(2)}, u32[]{:S(2)}) collective-permute-start(bf16[2,512,512]{1,2,0:T(8,128)(2,1)S(1)} %get-tuple-element.181), channel_id=1, source_target_pairs={{0,4},{4,8},{8,12},{1,5},{5,9},{9,13},{2,6},{6,10},{10,14},{3,7},{... | collective-permute-start | bytes 3145736 | tf_op jit(solution)/shard_map/ppermute | solution.py:20
  178.0 7.9 %copy-start.1 = (s32[2,1024]{1,0:T(2,128)S(1)}, s32[2,1024]{1,0:T(2,128)}, u32[]{:S(2)}) copy-start(s32[2,1024]{1,0:T(2,128)} %param.11) | copy-start | bytes 24580
  178.0 7.9 %copy-start.4 = (s32[8]{0:T(128)S(1)}, s32[8]{0:T(128)}, u32[]{:S(2)}) copy-start(s32[8]{0:T(128)} %param.12) | copy-start | bytes 100
  220.7 11.4 %copy-start.5 = (bf16[512,8,64]{0,2,1:T(8,128)(2,1)S(1)}, bf16[512,8,64]{0,2,1:T(8,128)(2,1)}, u32[]{:S(2)}) copy-start(bf16[512,8,64]{0,2,1:T(8,128)(2,1)} %get-tuple-element.311) | copy-start | bytes 1572868 | tf_op jit(solution)/shard_map/while
  232.0 1.9 copy-start.2
  234.0 1.0 copy-start.3
  269.6 11.4 %copy-start.5 = (bf16[512,8,64]{0,2,1:T(8,128)(2,1)S(1)}, bf16[512,8,64]{0,2,1:T(8,128)(2,1)}, u32[]{:S(2)}) copy-start(bf16[512,8,64]{0,2,1:T(8,128)(2,1)} %get-tuple-element.311) | copy-start | bytes 1572868 | tf_op jit(solution)/shard_map/while
  280.9 1.9 copy-start.2
  282.9 1.0 copy-start.3
Sparse Core Ops, SparseCore 0:
  10.1 24.3 reduce-scatter.1
  89.3 50.7 all-reduce.1
  142.3 21.9 all-gather.1
